TPU v7x, 256 devices: a whole 4x4x8 slice. The times are simulated.
256 devices in a mesh: stream: 32 (over y, x, core), span: 8 (over z).
Axes of the slice: x: 4, y: 4, z: 8, core: 2. Of those that a mesh axis runs over, the one named last changes fastest.
Arguments:
- solution: float32 [512, 128, 128], P('stream', 'span'), may hold values from -6 to 6
- residual: float32 [512, 128, 128], P('stream', 'span'), may hold values from -6 to 6
- direction: float32 [512, 128, 128], P('stream', 'span'), may hold values from -6 to 6
- rz_old: float32 [1], replicated, may hold values from 838860.8 to 3355443.2
- wall_flags: int32 [2, 512, 128], P(None, 'stream', 'span'), may hold values 0 or 1
- owner_list: int32 [256], P(('stream', 'span')), may hold values from 0 to 15
- coarse_basis: bfloat16 [64, 512, 128, 128], P(None, 'stream', 'span'), may hold values from -0.09375 to 0.09375
- coarse_inverse: float32 [1024, 1024], replicated, as said below
Outputs:
- new_solution: float32 [512, 128, 128], P('stream', 'span')
- new_residual: float32 [512, 128, 128], P('stream', 'span')
- new_direction: float32 [512, 128, 128], P('stream', 'span')
Inputs may be any that keep to these rules, and one draw needn't show every extreme that they name: `coarse_inverse`: symmetric positive definite.
All inputs are finite; a program needn't handle non-finite values. No bound on the sum of `wall_flags` on one device may be relied on, other than what follows from the above.
Results may differ from a plain program's by a relative error of at most 0.0015.
The roundings to bfloat16 on the way count: a program that leaves them out, or rounds other values in their place, can miss the bound.
Values sent between devices are 32-bit elements; how exact they have to be, the bound alone decides.
A program may use at most 64 MiB of HBM per device.

v0:
```python
import jax
import jax.numpy as jnp
from jax import lax
from jax.sharding import PartitionSpec as P


def extended(block, sides, width, periodic):
    for axis, dim in sides:
        count = lax.axis_size(axis)
        forward = [(i, i + 1) for i in range(count - 1)]
        if periodic:
            forward.append((count - 1, 0))
        backward = [(target, source) for source, target in forward]
        low = lax.ppermute(
            lax.slice_in_dim(block, block.shape[dim] - width, None, axis=dim), axis, forward
        )
        high = lax.ppermute(lax.slice_in_dim(block, 0, width, axis=dim), axis, backward)
        block = jnp.concatenate([low, block, high], axis=dim)
    return block


def on_device(
    solution, residual, direction, rz_old, wall_flags, owner_list, coarse_basis, coarse_inverse
):
    depth = direction.shape[2]
    stream_pad = extended(direction, (("stream", 0),), 1, True)
    span_pad = extended(direction, (("span", 1),), 1, False)
    low_keep = (1 - wall_flags[0]).astype(jnp.float32)[:, :, None]
    top_keep = (1 - wall_flags[1]).astype(jnp.float32)[:, :, None]
    z_padded = jnp.concatenate(
        [direction[:, :, :1] * low_keep, direction, direction[:, :, -1:] * top_keep], 2
    )
    neighbor_sum = stream_pad[2:] + stream_pad[:-2] + span_pad[:, 2:] + span_pad[:, :-2]
    neighbor_sum = neighbor_sum + z_padded[:, :, 2:] + z_padded[:, :, :-2]
    applied = 6.0 * direction - neighbor_sum
    basis_count = coarse_basis.shape[0]
    aggregates = coarse_inverse.shape[0] // basis_count
    flat_basis = coarse_basis.reshape(basis_count, -1)
    both_low = jnp.stack(
        [residual.astype(jnp.bfloat16).reshape(-1), applied.astype(jnp.bfloat16).reshape(-1)], 1
    )
    projected = jnp.dot(flat_basis, both_low, preferred_element_type=jnp.float32)
    selector = (jnp.arange(aggregates, dtype=jnp.int32) == owner_list[0]).astype(jnp.float32)
    local_curv = jnp.sum(direction * applied)
    total_curv = lax.psum(local_curv, ("stream", "span"))
    step_size = rz_old[0] / total_curv
    coarse_res = projected[:, 0] - step_size * projected[:, 1]
    coarse_rhs = lax.psum(selector[:, None] * coarse_res[None, :], ("stream", "span"))
    new_solution = solution + step_size * direction
    new_residual = residual - step_size * applied
    coarse_sol = jnp.dot(
        coarse_inverse, coarse_rhs.reshape(-1), precision=lax.Precision.HIGHEST
    ).reshape(aggregates, basis_count)
    own_coarse = jnp.dot(selector, coarse_sol, precision=lax.Precision.HIGHEST).astype(jnp.bfloat16)
    correction = jnp.dot(own_coarse, flat_basis, preferred_element_type=jnp.float32).reshape(
        direction.shape
    )
    level = jnp.arange(depth)
    low_mask = (level == 0).astype(jnp.float32)
    top_mask = (level == depth - 1).astype(jnp.float32)
    diagonal_vals = 6.0 - low_keep * low_mask - top_keep * top_mask
    precond = new_residual / diagonal_vals + correction
    rz_new = lax.psum(jnp.sum(new_residual * precond), ("stream", "span"))
    new_direction = precond + rz_new / rz_old[0] * direction
    return (new_solution, new_residual, new_direction)


def solution(mesh):
    in_specs = (
        P("stream", "span", None),
        P("stream", "span", None),
        P("stream", "span", None),
        P(),
        P(None, "stream", "span"),
        P(("stream", "span")),
        P(None, "stream", "span", None),
        P(),
    )
    out_specs = (P("stream", "span", None), P("stream", "span", None), P("stream", "span", None))
    return jax.shard_map(
        on_device, mesh=mesh, in_specs=in_specs, out_specs=out_specs, check_vma=False
    )
```

profile of v0, /device:TPU:1, one launch (start us, length us, event | category | flops | bytes accessed | tf_op | source)
XLA Modules:
  0.0 272.4 jit_solution(4774252832037127518)
XLA Ops:
  0.6 0.7 fusion.26
  1.3 3.2 %collective-permute-start = (f32[1,16,128]{2,1,0:T(8,128)S(1)}, f32[1,16,128]{2,1,0:T(8,128)S(1)}, u32[]{:S(2)}, u32[]{:S(2)}) collective-permute-start(f32[1,16,128]{2,1,0:T(8,128)S(1)} %get-tuple-element.9), channel_id=1, source_target_pairs={{8,0},{16,8},{24,16},{32,24},{40,32},{48,40},{56,48},{64,56},{72,6... | collective-permute-start | bytes 24584 | tf_op jit(solution)/shard_map/ppermute | solution.py:17
  4.6 0.0 collective-permute-start.1
  4.6 0.9 fusion.27
  5.5 1.3 collective-permute-start.2
  6.8 4.0 %collective-permute-start.3 = (f32[16,1,128]{2,1,0:T(1,128)S(1)}, f32[16,1,128]{2,1,0:T(1,128)S(1)}, u32[]{:S(2)}, u32[]{:S(2)}) collective-permute-start(f32[16,1,128]{2,1,0:T(1,128)S(1)} %get-tuple-element.12), channel_id=1, source_target_pairs={{0,1},{1,2},{2,3},{3,4},{4,5},{5,6},{6,7},{8,9},{9,10},{10,11},{11... | collective-permute-start | bytes 24584 | tf_op jit(solution)/shard_map/ppermute | solution.py:14
  10.8 1.1 fusion.28
  11.9 0.1 copy.21
  12.0 0.2 copy.22
  12.9 0.7 convert_bitcast_fusion
  13.6 0.7 bitcast_multiply_fusion.1
  14.3 0.2 copy.14
  14.5 0.2 copy.16
  15.3 0.9 convert_element_type.73
  16.2 0.0 copy-start.1
  16.3 4.9 %copy.34 = bf16[8,8,256,128]{3,1,2,0:T(8,128)(2,1)S(1)} copy(bf16[8,8,256,128]{3,2,1,0:T(8,128)(2,1)} %bitcast.60) | data formatting | bytes 8388608
  21.2 0.0 collective-permute-done
  21.2 0.0 collective-permute-done.1
  21.2 0.0 collective-permute-done.2
  21.2 0.0 collective-permute-done.3
  21.2 0.0 copy-done.1
  21.2 0.2 fusion.24
  21.4 0.6 multiply_reduce_fusion.1
  22.1 3.1 %copy.24 = bf16[8,8,256,128]{3,2,1,0:T(8,128)(2,1)} copy(bf16[8,8,256,128]{3,1,2,0:T(8,128)(2,1)S(1)} %copy.34) | data formatting | bytes 8388608
  25.2 82.5 %psum.21 = f32[]{:T(128)} all-reduce(f32[]{:T(128)} %multiply_reduce_fusion.1), channel_id=1, replica_groups=mesh['stream'=32,'span'=8] {'stream','span'}, use_global_device_ids=true, to_apply=%region_1.0 | all-reduce | flops 1 | bytes 8 | tf_op jit(solution)/shard_map/psum | solution.py:45
  108.4 6.0 %fusion.5 = f32[64,2]{0,1:T(2,128)S(1)} fusion(bf16[8,8,256,128]{3,2,1,0:T(8,128)(2,1)} %bitcast.61, bf16[32768,1]{0,1:T(2,128)(2,1)S(1)} %stack_reshape.7, bf16[32768,1]{0,1:T(2,128)(2,1)S(1)} %stack_reshape.6), kind=kOutput, calls=%fused_computation.6 | convolution fusion | flops 8650752 | bytes 4325888 | tf_op jit(solution)/shard_map/dot_general | solution.py:42
  114.3 0.1 broadcast_multiply_fusion
  114.4 0.1 reshape.85
  114.5 73.1 %psum.22 = f32[1024]{0:T(1024)S(1)} all-reduce(f32[1024]{0:T(1024)S(1)} %reshape.85), channel_id=1, replica_groups=mesh['stream'=32,'span'=8] {'stream','span'}, use_global_device_ids=true, to_apply=%region_2.0 | all-reduce | flops 1024 | bytes 8192 | tf_op jit(solution)/shard_map/psum | solution.py:48
  187.6 0.0 copy-start
  187.6 0.0 copy-start.3
  187.6 0.0 copy-start.4
  187.6 6.9 %fusion.29 = f32[1,16,64]{2,0,1:T(1,128)S(1)} fusion(f32[1024,1,1]{0,1,2:T(1,128)S(1)} %bitcast.65, f32[16,64,1024]{2,1,0:T(8,128)} %bitcast.59), kind=kOutput, calls=%fused_computation.51 | convolution fusion | flops 12582912 | bytes 4202496 | tf_op jit(solution)/shard_map/dot_general | solution.py:51
  194.5 0.1 fusion.9
  194.6 0.0 copy-done
  194.6 2.4 fusion.2
  197.0 0.0 copy-done.3
  197.0 0.8 multiply_reduce_fusion
  197.8 0.0 copy-start.2
  197.8 73.2 %psum.23 = f32[]{:T(128)} all-reduce(f32[]{:T(128)} %get-tuple-element.3), channel_id=1, replica_groups=mesh['stream'=32,'span'=8] {'stream','span'}, use_global_device_ids=true, to_apply=%region_4.0 | all-reduce | flops 1 | bytes 8 | tf_op jit(solution)/shard_map/psum | solution.py:63
  271.6 0.0 copy-done.4
  271.6 0.8 multiply_add_fusion
  272.4 0.0 copy-done.2
  (5 shorter events, 0.1 us)
Async XLA Ops:
  1.3 19.9 %collective-permute-start = (f32[1,16,128]{2,1,0:T(8,128)S(1)}, f32[1,16,128]{2,1,0:T(8,128)S(1)}, u32[]{:S(2)}, u32[]{:S(2)}) collective-permute-start(f32[1,16,128]{2,1,0:T(8,128)S(1)} %get-tuple-element.9), channel_id=1, source_target_pairs={{8,0},{16,8},{24,16},{32,24},{40,32},{48,40},{56,48},{64,56},{72,6... | collective-permute-start | bytes 24584 | tf_op jit(solution)/shard_map/ppermute | solution.py:17
  4.6 16.6 %collective-permute-start.1 = (f32[1,16,128]{2,1,0:T(8,128)S(1)}, f32[1,16,128]{2,1,0:T(8,128)S(1)}, u32[]{:S(2)}, u32[]{:S(2)}) collective-permute-start(f32[1,16,128]{2,1,0:T(8,128)S(1)} %get-tuple-element.10), channel_id=1, source_target_pairs={{0,8},{8,16},{16,24},{24,32},{32,40},{40,48},{48,56},{56,64},{64,7... | collective-permute-start | bytes 24584 | tf_op jit(solution)/shard_map/ppermute | solution.py:14
  5.5 15.7 %collective-permute-start.2 = (f32[16,1,128]{2,1,0:T(1,128)S(1)}, f32[16,1,128]{2,1,0:T(1,128)S(1)}, u32[]{:S(2)}, u32[]{:S(2)}) collective-permute-start(f32[16,1,128]{2,1,0:T(1,128)S(1)} %get-tuple-element.11), channel_id=1, source_target_pairs={{1,0},{2,1},{3,2},{4,3},{5,4},{6,5},{7,6},{9,8},{10,9},{11,10},{12... | collective-permute-start | bytes 24584 | tf_op jit(solution)/shard_map/ppermute | solution.py:17
  6.8 14.5 %collective-permute-start.3 = (f32[16,1,128]{2,1,0:T(1,128)S(1)}, f32[16,1,128]{2,1,0:T(1,128)S(1)}, u32[]{:S(2)}, u32[]{:S(2)}) collective-permute-start(f32[16,1,128]{2,1,0:T(1,128)S(1)} %get-tuple-element.12), channel_id=1, source_target_pairs={{0,1},{1,2},{2,3},{3,4},{4,5},{5,6},{6,7},{8,9},{9,10},{10,11},{11... | collective-permute-start | bytes 24584 | tf_op jit(solution)/shard_map/ppermute | solution.py:14
  16.2 5.0 %copy-start.1 = (f32[16,16,128]{2,1,0:T(8,128)S(1)}, f32[16,16,128]{2,1,0:T(8,128)}, u32[]{:S(2)}) copy-start(f32[16,16,128]{2,1,0:T(8,128)} %param.10) | copy-start | bytes 393220
  187.6 7.0 %copy-start = (bf16[8,8,256,128]{3,2,1,0:T(8,128)(2,1)S(1)}, bf16[8,8,256,128]{3,2,1,0:T(8,128)(2,1)}, u32[]{:S(2)}) copy-start(bf16[8,8,256,128]{3,2,1,0:T(8,128)(2,1)} %copy.24) | copy-start | bytes 12582916
  187.6 9.4 %copy-start.3 = (f32[16,16,128]{2,1,0:T(8,128)S(1)}, f32[16,16,128]{2,1,0:T(8,128)}, u32[]{:S(2)}) copy-start(f32[16,16,128]{2,1,0:T(8,128)} %param.9) | copy-start | bytes 393220
  187.6 84.0 %copy-start.4 = (f32[16,16,128]{2,1,0:T(8,128)S(1)}, f32[16,16,128]{2,1,0:T(8,128)}, u32[]{:S(2)}) copy-start(f32[16,16,128]{2,1,0:T(8,128)} %param.8) | copy-start | bytes 393220
  197.8 74.7 %copy-start.2 = (f32[16,16,128]{2,1,0:T(8,128)}, f32[16,16,128]{2,1,0:T(8,128)S(1)}, u32[]{:S(2)}) copy-start(f32[16,16,128]{2,1,0:T(8,128)S(1)} %get-tuple-element.4) | copy-start | bytes 393220
where the time goes:
time: 274 us; the launch traced here: 272 us
  blocking collectives  229 us (84%)
  matrix products  15.3 us (6%)
  local copies, waits for them, and re-layouts  11.5 us (4%)
  starting transfers between devices  8.52 us (3%)
  other arithmetic  4.81 us (2%)
  between operations  3.44 us (1%)
    psum x1, blocking collectives, on_device(): total_curv = lax.psum(local_curv, ('stream', 'span'))  82.5 us
    psum x1, blocking collectives, on_device(): rz_new = lax.psum(jnp.sum(new_residual * precond), ('stream', 'span'))  73.2 us
    psum x1, blocking collectives, on_device(): lax.psum(selector[:, None] * coarse_res[None, :], ('stream', 'span'))  73.1 us
    unnamed x14, local copies, waits for them, and re-layouts  8.37 us
    dot_general x1, matrix products, on_device(): jnp.dot(coarse_inverse, coarse_rhs.reshape(-1), precision=lax.Precision.H...  6.89 us
    dot_general x1, matrix products, on_device(): jnp.dot(flat_basis, both_low, preferred_element_type=jnp.float32)  5.96 us
  transfers between devices with their start and end apart: 4, of which 0 were waited for; matrix products, arithmetic and copies ran while one was open for 4% of the time, Pallas kernels for 0%

commit v1 on v0

v1 whole, which is shorter than its diff:
```python
import jax
import jax.numpy as jnp
from jax import lax
from jax.experimental import pallas as pl
from jax.experimental.pallas import tpu as pltpu
from jax.sharding import PartitionSpec as P

MESH = pl.DeviceIdType.MESH
F32 = jnp.float32
BF16 = jnp.bfloat16
NT = (((1,), (1,)), ((), ()))


def iota(shape, dim):
    return lax.broadcasted_iota(jnp.int32, shape, dim)


def split3(value):
    first = value.astype(BF16)
    rest = value - first.astype(F32)
    second = rest.astype(BF16)
    third = (rest - second.astype(F32)).astype(BF16)
    return first, second, third


def places():
    stream, z = lax.axis_index("stream"), lax.axis_index("span")
    y, x, core = stream // 8, lax.rem(stream // 2, 4), lax.rem(stream, 2)
    halo = [
        (lax.rem(stream + 1, 32), z),
        (lax.rem(stream + 31, 32), z),
        (stream, lax.rem(z + 1, 8)),
        (stream, lax.rem(z + 7, 8)),
    ]
    line = [
        ((y * 4 + x) * 2 + lax.rem(core + other, 2), lax.rem(z + away, 8))
        for away in (4, 3, 5, 2, 6, 1, 7, 0)
        for other in range(2)
        if away or other
    ]
    plane = [
        ((lax.rem(y + away // 4, 4) * 4 + lax.rem(x + away % 4, 4)) * 2 + core, z)
        for away in (10, 9, 11, 6, 14, 2, 8, 5, 7, 13, 15, 1, 3, 4, 12)
    ]
    return halo, line, plane, z * 2 + core, y * 4 + x, z


def kernel(
    sol_hbm, res_hbm, dir_hbm, rz_hbm, wall_hbm, own_hbm, basis_hbm, inv_hbm,
    new_sol, new_res, new_dir,
    sol, res, dirn, rz, wall, own, basis, inv,
    low_face, high_face, halo_buf, app, inv_diag, w_res, w_app, group_sum, part_res, v_ref,
    line_buf, plane_buf,
    in_sem, basis_sem, halo_send, halo_recv, line_send, line_recv, plane_send, plane_recv,
):
    halo, line, plane, line_me, plane_me, z = places()
    barrier = pltpu.get_barrier_semaphore()
    for peer in halo + line + plane:
        pl.semaphore_signal(barrier, inc=1, device_id=peer, device_id_type=MESH)
    loads = [
        pltpu.make_async_copy(src, dst, in_sem.at[i])
        for i, (src, dst) in enumerate(
            ((dir_hbm, dirn), (wall_hbm, wall), (res_hbm, res), (rz_hbm, rz), (own_hbm, own), (sol_hbm, sol), (inv_hbm, inv))
        )
    ]
    basis_loads = [
        pltpu.make_async_copy(basis_hbm.at[pl.ds(8 * i, 8)], basis.at[pl.ds(8 * i, 8)], basis_sem.at[i])
        for i in range(8)
    ]
    for load in loads[:5] + basis_loads + loads[5:]:
        load.start()

    lane = iota((16, 128), 1)
    row = iota((16, 128), 0)
    group_sum[...] = (iota((1024, 128), 0) // 16 == iota((1024, 128), 1) % 64).astype(F32).astype(BF16)

    loads[0].wait()
    for x in range(16):
        low_face[pl.ds(x, 1), :] = dirn[x, pl.ds(0, 1), :]
        high_face[pl.ds(x, 1), :] = dirn[x, pl.ds(15, 1), :]
    pl.semaphore_wait(barrier, len(halo + line + plane))
    sends = []
    for i, (src, peer) in enumerate(zip((dirn.at[15], dirn.at[0], high_face, low_face), halo)):
        copy = pltpu.make_async_remote_copy(
            src_ref=src, dst_ref=halo_buf.at[i], send_sem=halo_send.at[i], recv_sem=halo_recv.at[i],
            device_id=peer, device_id_type=MESH,
        )
        copy.start()
        sends.append(copy)

    loads[1].wait()
    loads[2].wait()
    same = iota((16, 16), 0) == iota((16, 16), 1)
    keep_low = (1 - wall[0]).astype(F32)
    keep_top = (1 - wall[1]).astype(F32)
    sum_rr = jnp.zeros((16, 128), F32)
    for x in range(16):
        own_d = dirn[x]
        low = jnp.sum(jnp.where(same, keep_low[x : x + 1, :], 0.0), axis=1, keepdims=True)
        top = jnp.sum(jnp.where(same, keep_top[x : x + 1, :], 0.0), axis=1, keepdims=True)
        around = jnp.where(lane == 0, own_d * low, pltpu.roll(own_d, 1, 1))
        around += jnp.where(lane == 127, own_d * top, pltpu.roll(own_d, 127, 1))
        around += jnp.where(row == 0, 0.0, pltpu.roll(own_d, 1, 0))
        around += jnp.where(row == 15, 0.0, pltpu.roll(own_d, 15, 0))
        if x > 0:
            around += dirn[x - 1]
        if x < 15:
            around += dirn[x + 1]
        app[x] = 6.0 * own_d - around
        diag = 6.0 - jnp.where(lane == 0, low, 0.0) - jnp.where(lane == 127, top, 0.0)
        inverse = 1.0 / diag
        inv_diag[x] = inverse
        r = res[x]
        sum_rr += r * r * inverse
        r_low = r.astype(BF16)
        w_res[0:16, 128 * x : 128 * x + 128] = r_low
        w_res[16:32, 128 * x : 128 * x + 128] = (r - r_low.astype(F32)).astype(BF16)

    pick = iota((32, 1024), 0) % 16 == iota((32, 1024), 1) % 16

    def slab(pair):
        return jnp.concatenate(
            [basis[:, 2 * pair].reshape(1024, 128), basis[:, 2 * pair + 1].reshape(1024, 128)], axis=1
        )

    def project(weights):
        total = jnp.zeros((32, 1024), F32)
        for pair in range(8):
            total += lax.dot_general(
                weights[:, 256 * pair : 256 * pair + 256], slab(pair), NT, preferred_element_type=F32
            )
        total = jnp.where(pick, total, 0.0)
        first = jnp.sum(total[0:16], axis=0, keepdims=True)
        second = jnp.sum(total[16:32], axis=0, keepdims=True)
        at = iota((8, 1024), 0)
        both = jnp.where(at == 0, first, jnp.where(at == 1, second, 0.0))
        one, two, three = (part.astype(F32) for part in split3(both))
        stacked = jnp.concatenate([one, two, three, jnp.zeros_like(one)], axis=0).astype(BF16)
        sums = jnp.dot(stacked, group_sum[...], preferred_element_type=F32)
        return sums[0:8] + sums[8:16] + sums[16:24]

    for load in basis_loads:
        load.wait()
    part_res[...] = project(w_res)

    for copy in sends:
        copy.wait_recv()
    from_low = jnp.where(z > 0, 1.0, 0.0)
    from_high = jnp.where(z < 7, 1.0, 0.0)
    sum_dq = jnp.zeros((16, 128), F32)
    sum_rq = jnp.zeros((16, 128), F32)
    sum_qq = jnp.zeros((16, 128), F32)
    for x in range(16):
        q = app[x]
        if x == 0:
            q -= halo_buf[0]
        if x == 15:
            q -= halo_buf[1]
        q -= jnp.where(row == 0, halo_buf[2, pl.ds(x, 1), :] * from_low, 0.0)
        q -= jnp.where(row == 15, halo_buf[3, pl.ds(x, 1), :] * from_high, 0.0)
        app[x] = q
        scaled = q * inv_diag[x]
        sum_dq += dirn[x] * q
        sum_rq += res[x] * scaled
        sum_qq += q * scaled
        q_low = q.astype(BF16)
        w_app[0:16, 128 * x : 128 * x + 128] = q_low
        w_app[16:32, 128 * x : 128 * x + 128] = (q - q_low.astype(F32)).astype(BF16)
    part_app = project(w_app)
    loads[4].wait()
    lane1 = lane[0:1]
    scalars = own[0].astype(F32) * jnp.where(lane1 == 4, 1.0, 0.0)
    for i, value in enumerate((sum_dq, sum_rr, sum_rq, sum_qq)):
        whole = jnp.sum(jnp.sum(value, axis=0, keepdims=True), axis=1, keepdims=True)
        scalars = jnp.where(lane1 == i, whole, scalars)
    line_buf[line_me, pl.ds(0, 1), :] = jnp.where(lane1 < 64, part_res[0:1, :], part_app[0:1, :])
    line_buf[line_me, pl.ds(1, 1), :] = jnp.where(lane1 < 64, part_res[1:2, :], part_app[1:2, :])
    line_buf[line_me, pl.ds(2, 1), :] = scalars

    copies = []
    for i, peer in enumerate(line):
        copy = pltpu.make_async_remote_copy(
            src_ref=line_buf.at[line_me], dst_ref=line_buf.at[line_me], send_sem=line_send.at[i],
            recv_sem=line_recv.at[i], device_id=peer, device_id_type=MESH,
        )
        copy.start()
        copies.append(copy)
    sends += copies
    for copy in copies:
        copy.wait_recv()
    rows = pl.ds(pl.multiple_of(plane_me * 16, 16), 16)
    for kind in range(3):
        plane_buf[kind, rows, :] = line_buf[:, kind, :]
    copies = []
    for i, peer in enumerate(plane):
        copy = pltpu.make_async_remote_copy(
            src_ref=plane_buf.at[:, rows], dst_ref=plane_buf.at[:, rows], send_sem=plane_send.at[i],
            recv_sem=plane_recv.at[i], device_id=peer, device_id_type=MESH,
        )
        copy.start()
        copies.append(copy)
    sends += copies
    loads[3].wait()
    loads[5].wait()
    loads[6].wait()
    for copy in copies:
        copy.wait_recv()

    flat = plane_buf[2]
    totals = jnp.sum(flat, axis=0, keepdims=True)
    rz_old = rz[0]
    step = rz_old / totals[:, 0:1]
    for x in range(16):
        new_sol[x] = sol[x] + step * dirn[x]
    owners = lax.dot_general(
        jnp.ones((16, 128), BF16), jnp.where(iota((256, 128), 1) == 4, flat, 0.0).astype(BF16), NT,
        preferred_element_type=F32,
    )
    at = iota((16, 256), 0)
    wanted = jnp.where(at < 8, 2 * at, 2 * at - 15).astype(F32)
    chosen = (owners == wanted).astype(F32).astype(BF16)
    sums = jnp.zeros((16, 256), F32)
    for part in split3(jnp.concatenate([plane_buf[0], plane_buf[1]], axis=1)):
        sums += jnp.dot(chosen, part, preferred_element_type=F32)
    lane8 = iota((8, 128), 1)
    row8 = iota((8, 128), 0)

    def coarse(even, odd):
        return jnp.where(
            lane8 < 64, even - step * pltpu.roll(even, 64, 1), pltpu.roll(odd, 64, 1) - step * odd
        )

    rhs = coarse(sums[0:8, 0:128], sums[8:16, 0:128])
    rhs_rest = coarse(sums[0:8, 128:256], sums[8:16, 128:256])
    v_ref[...] = rhs

    def block(tile, total):
        values = v_ref[pl.ds(tile, 1), :]
        for k in range(16):
            column = jnp.sum(jnp.where(lane8 == row8 + 8 * k, values, 0.0), axis=1, keepdims=True)
            total += column * inv[pl.ds(pl.multiple_of(tile * 128 + 8 * k, 8), 8), :]
        return total

    total = lax.fori_loop(0, 8, block, jnp.zeros((8, 1024), F32))
    answer = jnp.zeros((8, 128), F32)
    for tile in range(8):
        answer = jnp.where(
            row8 == tile, jnp.sum(total[:, 128 * tile : 128 * tile + 128], axis=0, keepdims=True), answer
        )
    answer = answer.astype(BF16).astype(F32)
    inner = jnp.sum(jnp.sum(answer * (rhs + rhs_rest), axis=0, keepdims=True), axis=1, keepdims=True)
    rz_new = totals[:, 1:2] - 2.0 * step * totals[:, 2:3] + step * step * totals[:, 3:4] + inner
    ratio = rz_new / rz_old
    mine = own[0]
    here = jnp.where(row8 == (mine >> 1), jnp.where((lane8 >> 6) == (mine & 1), answer, 0.0), 0.0)
    here = jnp.broadcast_to(jnp.sum(here, axis=0, keepdims=True), (16, 128)).astype(BF16)
    spread = lax.dot_general(here, group_sum[...], NT, preferred_element_type=F32)
    spread = jnp.where(pick[0:16], spread, 0.0).astype(BF16)
    for pair in range(8):
        correction = jnp.dot(spread, slab(pair), preferred_element_type=F32)
        for side in range(2):
            x = 2 * pair + side
            d = dirn[x]
            updated = res[x] - step * app[x]
            new_res[x] = updated
            new_dir[x] = updated * inv_diag[x] + correction[:, 128 * side : 128 * side + 128] + ratio * d
    for copy in sends:
        copy.wait_send()


def on_device(*args):
    block = jax.ShapeDtypeStruct((16, 16, 128), F32)
    return pl.pallas_call(
        kernel,
        out_shape=(block, block, block),
        in_specs=[pl.BlockSpec(memory_space=pltpu.HBM)] * 8,
        out_specs=(pl.BlockSpec(memory_space=pltpu.VMEM),) * 3,
        scratch_shapes=[
            pltpu.VMEM((16, 16, 128), F32),
            pltpu.VMEM((16, 16, 128), F32),
            pltpu.VMEM((16, 16, 128), F32),
            pltpu.SMEM((1,), F32),
            pltpu.VMEM((2, 16, 16), jnp.int32),
            pltpu.SMEM((1,), jnp.int32),
            pltpu.VMEM((64, 16, 16, 128), BF16),
            pltpu.VMEM((1024, 1024), F32),
            pltpu.VMEM((16, 128), F32),
            pltpu.VMEM((16, 128), F32),
            pltpu.VMEM((4, 16, 128), F32),
            pltpu.VMEM((16, 16, 128), F32),
            pltpu.VMEM((16, 16, 128), F32),
            pltpu.VMEM((32, 2048), BF16),
            pltpu.VMEM((32, 2048), BF16),
            pltpu.VMEM((1024, 128), BF16),
            pltpu.VMEM((8, 128), F32),
            pltpu.VMEM((8, 128), F32),
            pltpu.VMEM((16, 3, 128), F32),
            pltpu.VMEM((3, 256, 128), F32),
            pltpu.SemaphoreType.DMA((7,)),
            pltpu.SemaphoreType.DMA((8,)),
            pltpu.SemaphoreType.DMA((4,)),
            pltpu.SemaphoreType.DMA((4,)),
            pltpu.SemaphoreType.DMA((15,)),
            pltpu.SemaphoreType.DMA((15,)),
            pltpu.SemaphoreType.DMA((15,)),
            pltpu.SemaphoreType.DMA((15,)),
        ],
        compiler_params=pltpu.CompilerParams(
            collective_id=0, has_side_effects=True, vmem_limit_bytes=62 * 1024 * 1024
        ),
    )(*args)


def solution(mesh):
    field = P("stream", "span", None)
    in_specs = (
        field,
        field,
        field,
        P(),
        P(None, "stream", "span"),
        P(("stream", "span")),
        P(None, "stream", "span", None),
        P(),
    )
    return jax.shard_map(
        on_device, mesh=mesh, in_specs=in_specs, out_specs=(field, field, field), check_vma=False
    )
```

time: 274 us -> 37.2 us (0.14)
  blocking collectives: 229 us -> 0 us
  Pallas kernels: 0 us -> 30.4 us
  matrix products: 15.3 us -> 0 us
  starting transfers between devices: 8.52 us -> 0 us
  local copies, waits for them, and re-layouts: 11.5 us -> 4.7 us
  other arithmetic: 4.81 us -> 0 us
    psum x3 -> x0, blocking collectives: 229 us -> none  [the longest x1 82.5 us: on_device(): total_curv = lax.psum(local_curv, ('stream', 'span'))]
    pallas_call x0 -> x1, Pallas kernels: none -> 30.4 us  [on_device(): pl.pallas_call(kernel, out_shape=(block, block, block), in_specs=[pl.Bloc...]
    dot_general x4 -> x0, matrix products: 15.3 us -> none  [the longest x1 6.89 us: on_device(): jnp.dot(coarse_inverse, coarse_rhs.reshape(-1), precision=lax.Precision.H...]
    ppermute x4 -> x0, starting transfers between devices: 8.52 us -> none  [the longest x2 4.53 us: extended(): lax.ppermute(lax.slice_in_dim(block, 0, width, axis=dim), axis, backward)]
    unnamed x14 -> x3, local copies, waits for them, and re-layouts: 8.37 us -> 4.7 us
  transfers between devices with their start and end apart: 4 -> 0, of which waited for: 0 -> 0; matrix products, arithmetic and copies ran while one was open for 4% -> 0% of each run, Pallas kernels for 0% -> 0%
where the time goes in v1:
time: 37.2 us; the launch traced here: 37 us
  Pallas kernels  30.4 us (82%)
  local copies, waits for them, and re-layouts  4.7 us (13%)
  between operations  1.93 us (5%)
    pallas_call x1, Pallas kernels, on_device(): pl.pallas_call(kernel, out_shape=(block, block, block), in_specs=[pl.Bloc...  30.4 us
    unnamed x3, local copies, waits for them, and re-layouts  4.7 us

profile of v1, /device:TPU:1, one launch (start us, length us, event | category | flops | bytes accessed | tf_op | source)
XLA Modules:
  0.0 37.0 jit_solution(10775496881456845049)
XLA Ops:
  1.9 30.4 %shard_map.103 = (f32[16,16,128]{2,1,0:T(8,128)}, f32[16,16,128]{2,1,0:T(8,128)}, f32[16,16,128]{2,1,0:T(8,128)}) custom-call(f32[16,16,128]{2,1,0:T(8,128)} %sol_hbm.1, f32[16,16,128]{2,1,0:T(8,128)} %res_hbm.1, f32[16,16,128]{2,1,0:T(8,128)} %dir_hbm.1, f32[1]{0:T(128)S(6)} %copy.14.rz_hbm, s32[2,16,16]{2,1,0:T(8,128)} %wall_hbm.1, s32[1]{0:T(128)S(6)} %copy.15.own_hbm, ...), custom_call_target="tpu_custom_call" | custom-call | tf_op jit(solution)/shard_map/pallas_call | solution.py:273
  32.3 1.6 %copy.16 = f32[16,16,128]{2,1,0:T(8,128)} copy(f32[16,16,128]{2,1,0:T(8,128)} %get-tuple-element.6) | data formatting | bytes 262144
  33.9 1.6 %copy.17 = f32[16,16,128]{2,1,0:T(8,128)} copy(f32[16,16,128]{2,1,0:T(8,128)} %get-tuple-element.7) | data formatting | bytes 262144
  35.4 1.6 %copy.18 = f32[16,16,128]{2,1,0:T(8,128)} copy(f32[16,16,128]{2,1,0:T(8,128)} %get-tuple-element.8) | data formatting | bytes 262144

commit v2 on v1

--- a/solution.py
+++ b/solution.py
@@ -46,10 +46,10 @@
 
 
 def kernel(
-    sol_hbm, res_hbm, dir_hbm, rz_hbm, wall_hbm, own_hbm, basis_hbm, inv_hbm,
-    new_sol, new_res, new_dir,
-    sol, res, dirn, rz, wall, own, basis, inv,
-    low_face, high_face, halo_buf, app, inv_diag, w_res, w_app, group_sum, part_res, v_ref,
+    res_hbm, dir_hbm, rz_hbm, wall_hbm, own_hbm, basis_hbm, inv_hbm,
+    app, precond, step_row, ratio_row,
+    res, dirn, rz, wall, own, basis, inv,
+    low_face, high_face, halo_buf, inv_diag, w_res, w_app, group_sum, part_res, v_ref,
     line_buf, plane_buf,
     in_sem, basis_sem, halo_send, halo_recv, line_send, line_recv, plane_send, plane_recv,
 ):
@@ -60,7 +60,7 @@
     loads = [
         pltpu.make_async_copy(src, dst, in_sem.at[i])
         for i, (src, dst) in enumerate(
-            ((dir_hbm, dirn), (wall_hbm, wall), (res_hbm, res), (rz_hbm, rz), (own_hbm, own), (sol_hbm, sol), (inv_hbm, inv))
+            ((dir_hbm, dirn), (wall_hbm, wall), (res_hbm, res), (rz_hbm, rz), (own_hbm, own), (inv_hbm, inv))
         )
     ]
     basis_loads = [
@@ -169,7 +169,7 @@
     part_app = project(w_app)
     loads[4].wait()
     lane1 = lane[0:1]
-    scalars = own[0].astype(F32) * jnp.where(lane1 == 4, 1.0, 0.0)
+    scalars = own[0, 0].astype(F32) * jnp.where(lane1 == 16 + line_me, 1.0, 0.0)
     for i, value in enumerate((sum_dq, sum_rr, sum_rq, sum_qq)):
         whole = jnp.sum(jnp.sum(value, axis=0, keepdims=True), axis=1, keepdims=True)
         scalars = jnp.where(lane1 == i, whole, scalars)
@@ -188,13 +188,13 @@
     sends += copies
     for copy in copies:
         copy.wait_recv()
-    rows = pl.ds(pl.multiple_of(plane_me * 16, 16), 16)
-    for kind in range(3):
-        plane_buf[kind, rows, :] = line_buf[:, kind, :]
+    for kind in range(2):
+        plane_buf[plane_me, pl.ds(16 * kind, 16), :] = line_buf[:, kind, :]
+    plane_buf[plane_me, pl.ds(32, 1), :] = jnp.sum(line_buf[:, 2, :], axis=0, keepdims=True)
     copies = []
     for i, peer in enumerate(plane):
         copy = pltpu.make_async_remote_copy(
-            src_ref=plane_buf.at[:, rows], dst_ref=plane_buf.at[:, rows], send_sem=plane_send.at[i],
+            src_ref=plane_buf.at[plane_me], dst_ref=plane_buf.at[plane_me], send_sem=plane_send.at[i],
             recv_sem=plane_recv.at[i], device_id=peer, device_id_type=MESH,
         )
         copy.start()
@@ -202,25 +202,23 @@
     sends += copies
     loads[3].wait()
     loads[5].wait()
-    loads[6].wait()
     for copy in copies:
         copy.wait_recv()
 
-    flat = plane_buf[2]
-    totals = jnp.sum(flat, axis=0, keepdims=True)
-    rz_old = rz[0]
+    scalars = plane_buf[:, 32, :]
+    totals = jnp.sum(scalars, axis=0, keepdims=True)
+    rz_old = rz[0, 0]
     step = rz_old / totals[:, 0:1]
-    for x in range(16):
-        new_sol[x] = sol[x] + step * dirn[x]
-    owners = lax.dot_general(
-        jnp.ones((16, 128), BF16), jnp.where(iota((256, 128), 1) == 4, flat, 0.0).astype(BF16), NT,
-        preferred_element_type=F32,
-    )
+    step_row[0] = jnp.broadcast_to(step, (1, 128))
+    to_lanes = (iota((128, 256), 0) == 16 + iota((128, 256), 1) % 16).astype(F32).astype(BF16)
+    owners = jnp.dot(jnp.where((lane >= 16) & (lane < 32), scalars, 0.0).astype(BF16), to_lanes, preferred_element_type=F32)
+    owners = jnp.where(iota((16, 256), 0) == iota((16, 256), 1) // 16, owners, 0.0)
+    owners = jnp.sum(owners, axis=0, keepdims=True)
     at = iota((16, 256), 0)
     wanted = jnp.where(at < 8, 2 * at, 2 * at - 15).astype(F32)
     chosen = (owners == wanted).astype(F32).astype(BF16)
     sums = jnp.zeros((16, 256), F32)
-    for part in split3(jnp.concatenate([plane_buf[0], plane_buf[1]], axis=1)):
+    for part in split3(jnp.concatenate([plane_buf[:, 0:16].reshape(256, 128), plane_buf[:, 16:32].reshape(256, 128)], axis=1)):
         sums += jnp.dot(chosen, part, preferred_element_type=F32)
     lane8 = iota((8, 128), 1)
     row8 = iota((8, 128), 0)
@@ -251,7 +249,8 @@
     inner = jnp.sum(jnp.sum(answer * (rhs + rhs_rest), axis=0, keepdims=True), axis=1, keepdims=True)
     rz_new = totals[:, 1:2] - 2.0 * step * totals[:, 2:3] + step * step * totals[:, 3:4] + inner
     ratio = rz_new / rz_old
-    mine = own[0]
+    ratio_row[0] = jnp.broadcast_to(ratio, (1, 128))
+    mine = own[0, 0]
     here = jnp.where(row8 == (mine >> 1), jnp.where((lane8 >> 6) == (mine & 1), answer, 0.0), 0.0)
     here = jnp.broadcast_to(jnp.sum(here, axis=0, keepdims=True), (16, 128)).astype(BF16)
     spread = lax.dot_general(here, group_sum[...], NT, preferred_element_type=F32)
@@ -260,34 +259,31 @@
         correction = jnp.dot(spread, slab(pair), preferred_element_type=F32)
         for side in range(2):
             x = 2 * pair + side
-            d = dirn[x]
             updated = res[x] - step * app[x]
-            new_res[x] = updated
-            new_dir[x] = updated * inv_diag[x] + correction[:, 128 * side : 128 * side + 128] + ratio * d
+            precond[x] = updated * inv_diag[x] + correction[:, 128 * side : 128 * side + 128]
     for copy in sends:
         copy.wait_send()
 
 
-def on_device(*args):
-    block = jax.ShapeDtypeStruct((16, 16, 128), F32)
-    return pl.pallas_call(
+def on_device(solution, residual, direction, rz_old, wall_flags, owner_list, coarse_basis, coarse_inverse):
+    block = pltpu.VMEM((16, 16, 128), F32)
+    line = pltpu.VMEM((1, 1, 128), F32)
+    applied, precond, step, ratio = pl.pallas_call(
         kernel,
-        out_shape=(block, block, block),
-        in_specs=[pl.BlockSpec(memory_space=pltpu.HBM)] * 8,
-        out_specs=(pl.BlockSpec(memory_space=pltpu.VMEM),) * 3,
+        out_shape=(block, block, line, line),
+        in_specs=[pl.BlockSpec(memory_space=pltpu.HBM)] * 7,
+        out_specs=(pl.BlockSpec(memory_space=pltpu.VMEM),) * 4,
         scratch_shapes=[
             pltpu.VMEM((16, 16, 128), F32),
             pltpu.VMEM((16, 16, 128), F32),
-            pltpu.VMEM((16, 16, 128), F32),
-            pltpu.SMEM((1,), F32),
+            pltpu.SMEM((1, 1), F32),
             pltpu.VMEM((2, 16, 16), jnp.int32),
-            pltpu.SMEM((1,), jnp.int32),
+            pltpu.SMEM((1, 1), jnp.int32),
             pltpu.VMEM((64, 16, 16, 128), BF16),
             pltpu.VMEM((1024, 1024), F32),
             pltpu.VMEM((16, 128), F32),
             pltpu.VMEM((16, 128), F32),
             pltpu.VMEM((4, 16, 128), F32),
-            pltpu.VMEM((16, 16, 128), F32),
             pltpu.VMEM((16, 16, 128), F32),
             pltpu.VMEM((32, 2048), BF16),
             pltpu.VMEM((32, 2048), BF16),
@@ -295,8 +291,8 @@
             pltpu.VMEM((8, 128), F32),
             pltpu.VMEM((8, 128), F32),
             pltpu.VMEM((16, 3, 128), F32),
-            pltpu.VMEM((3, 256, 128), F32),
-            pltpu.SemaphoreType.DMA((7,)),
+            pltpu.VMEM((16, 33, 128), F32),
+            pltpu.SemaphoreType.DMA((6,)),
             pltpu.SemaphoreType.DMA((8,)),
             pltpu.SemaphoreType.DMA((4,)),
             pltpu.SemaphoreType.DMA((4,)),
@@ -308,7 +304,8 @@
         compiler_params=pltpu.CompilerParams(
             collective_id=0, has_side_effects=True, vmem_limit_bytes=62 * 1024 * 1024
         ),
-    )(*args)
+    )(residual, direction, rz_old.reshape(1, 1), wall_flags, owner_list.reshape(1, 1), coarse_basis, coarse_inverse)
+    return solution + step * direction, residual - step * applied, precond + ratio * direction
 
 
 def solution(mesh):

time: 37.2 us -> 31.6 us (0.85)
  local copies, waits for them, and re-layouts: 4.7 us -> 0.01 us
  Pallas kernels: 30.4 us -> 28.7 us
  other arithmetic: 0 us -> 0.76 us
    unnamed x3 -> x6, local copies, waits for them, and re-layouts: 4.7 us -> 0.01 us
    pallas_call x1, Pallas kernels: 30.4 us -> 28.7 us  [on_device(): pl.pallas_call(kernel, out_shape=(block, block, line, line), in_specs=[pl...]
    add x0 -> x1, other arithmetic: none -> 0.76 us  [on_device(): precond + ratio * direction]
where the time goes in v2:
time: 31.6 us; the launch traced here: 31.5 us
  Pallas kernels  28.7 us (91%)
  between operations  1.98 us (6%)
  other arithmetic  0.76 us (2%)
    pallas_call x1, Pallas kernels, on_device(): pl.pallas_call(kernel, out_shape=(block, block, line, line), in_specs=[pl...  28.7 us
    add x1, other arithmetic, on_device(): precond + ratio * direction  0.76 us

profile of v2, /device:TPU:1, one launch (start us, length us, event | category | flops | bytes accessed | tf_op | source)
XLA Modules:
  0.0 31.5 jit_solution(15888320209341600109)
XLA Ops:
  1.9 0.0 copy-start
  1.9 0.0 copy-start.1
  1.9 0.0 copy-start.2
  2.0 28.7 %shard_map.103 = (f32[16,16,128]{2,1,0:T(8,128)S(1)}, f32[16,16,128]{2,1,0:T(8,128)S(1)}, f32[1,1,128]{2,1,0:T(1,128)S(1)}, f32[1,1,128]{2,1,0:T(1,128)S(1)}) custom-call(f32[16,16,128]{2,1,0:T(8,128)} %res_hbm.1, f32[16,16,128]{2,1,0:T(8,128)} %dir_hbm.1, f32[1,1]{1,0:T(1,128)} %bitcast.4.rz_hbm, s32[2,16,16]{2,1,0:T(8,128)} %wall_hbm.1, ...), custom_call_target="tpu_custom_call" | custom-call | tf_op jit(solution)/shard_map/pallas_call | solution.py:271
  30.7 0.0 copy-done
  30.7 0.0 copy-done.1
  30.7 0.0 copy-done.2
  30.7 0.8 %multiply_add_fusion = (f32[16,16,128]{2,1,0:T(8,128)}, f32[16,16,128]{2,1,0:T(8,128)}, f32[16,16,128]{2,1,0:T(8,128)}) fusion(f32[16,16,128]{2,1,0:T(8,128)S(1)} %get-tuple-element.9, f32[16,16,128]{2,1,0:T(8,128)S(1)} %copy-done.1, f32[128]{0:T(128)S(1)} %bitcast.7, f32[16,16,128]{2,1,0:T(8,128)S(1)} %copy-done.2, f32[128]{0:T(128)S(1)} %bitcast.6, ...), kind=kLoop, calls=%fused_computation | loop fusion | flops 196608 | bytes 1049600 | tf_op jit(solution)/shard_map/add | solution.py:308
Async XLA Ops:
  1.9 28.7 %copy-start = (f32[16,16,128]{2,1,0:T(8,128)S(1)}, f32[16,16,128]{2,1,0:T(8,128)}, u32[]{:S(2)}) copy-start(f32[16,16,128]{2,1,0:T(8,128)} %res_hbm.1) | copy-start | bytes 393220
  1.9 28.7 %copy-start.1 = (f32[16,16,128]{2,1,0:T(8,128)S(1)}, f32[16,16,128]{2,1,0:T(8,128)}, u32[]{:S(2)}) copy-start(f32[16,16,128]{2,1,0:T(8,128)} %dir_hbm.1) | copy-start | bytes 393220
  1.9 28.7 %copy-start.2 = (f32[16,16,128]{2,1,0:T(8,128)S(1)}, f32[16,16,128]{2,1,0:T(8,128)}, u32[]{:S(2)}) copy-start(f32[16,16,128]{2,1,0:T(8,128)} %param.8) | copy-start | bytes 393220

commit v3 on v2

--- a/solution.py
+++ b/solution.py
@@ -49,13 +49,13 @@
     res_hbm, dir_hbm, rz_hbm, wall_hbm, own_hbm, basis_hbm, inv_hbm,
     app, precond, step_row, ratio_row,
     res, dirn, rz, wall, own, basis, inv,
-    low_face, high_face, halo_buf, inv_diag, w_res, w_app, group_sum, part_res, v_ref,
+    low_face, high_face, halo_buf, inv_diag, w_res, w_app, group_sum, per_cell, part_res, v_ref,
     line_buf, plane_buf,
     in_sem, basis_sem, halo_send, halo_recv, line_send, line_recv, plane_send, plane_recv,
 ):
     halo, line, plane, line_me, plane_me, z = places()
     barrier = pltpu.get_barrier_semaphore()
-    for peer in halo + line + plane:
+    for peer in line[:2] + plane[:1] + line[2:6] + plane[1:5] + halo[:2] + line[6:10] + plane[5:] + line[10:] + halo[2:]:
         pl.semaphore_signal(barrier, inc=1, device_id=peer, device_id_type=MESH)
     loads = [
         pltpu.make_async_copy(src, dst, in_sem.at[i])
@@ -73,6 +73,7 @@
     lane = iota((16, 128), 1)
     row = iota((16, 128), 0)
     group_sum[...] = (iota((1024, 128), 0) // 16 == iota((1024, 128), 1) % 64).astype(F32).astype(BF16)
+    per_cell[...] = (iota((128, 1024), 0) % 64 == iota((128, 1024), 1) // 16).astype(F32).astype(BF16)
 
     loads[0].wait()
     for x in range(16):
@@ -239,7 +240,7 @@
             total += column * inv[pl.ds(pl.multiple_of(tile * 128 + 8 * k, 8), 8), :]
         return total
 
-    total = lax.fori_loop(0, 8, block, jnp.zeros((8, 1024), F32))
+    total = lax.fori_loop(0, 8, block, jnp.zeros((8, 1024), F32), unroll=True)
     answer = jnp.zeros((8, 128), F32)
     for tile in range(8):
         answer = jnp.where(
@@ -253,7 +254,7 @@
     mine = own[0, 0]
     here = jnp.where(row8 == (mine >> 1), jnp.where((lane8 >> 6) == (mine & 1), answer, 0.0), 0.0)
     here = jnp.broadcast_to(jnp.sum(here, axis=0, keepdims=True), (16, 128)).astype(BF16)
-    spread = lax.dot_general(here, group_sum[...], NT, preferred_element_type=F32)
+    spread = jnp.dot(here, per_cell[...], preferred_element_type=F32)
     spread = jnp.where(pick[0:16], spread, 0.0).astype(BF16)
     for pair in range(8):
         correction = jnp.dot(spread, slab(pair), preferred_element_type=F32)
@@ -288,6 +289,7 @@
             pltpu.VMEM((32, 2048), BF16),
             pltpu.VMEM((32, 2048), BF16),
             pltpu.VMEM((1024, 128), BF16),
+            pltpu.VMEM((128, 1024), BF16),
             pltpu.VMEM((8, 128), F32),
             pltpu.VMEM((8, 128), F32),
             pltpu.VMEM((16, 3, 128), F32),

time: 31.6 us -> 30 us (0.949)
  Pallas kernels: 28.7 us -> 27.2 us
    pallas_call x1, Pallas kernels: 28.7 us -> 27.2 us  [on_device(): pl.pallas_call(kernel, out_shape=(block, block, line, line), in_specs=[pl...]
where the time goes in v3:
time: 30 us; the launch traced here: 29.9 us
  Pallas kernels  27.2 us (91%)
  between operations  1.98 us (7%)
  other arithmetic  0.76 us (3%)
    pallas_call x1, Pallas kernels, on_device(): pl.pallas_call(kernel, out_shape=(block, block, line, line), in_specs=[pl...  27.2 us
    add x1, other arithmetic, on_device(): precond + ratio * direction  0.76 us

profile of v3, /device:TPU:1, one launch (start us, length us, event | category | flops | bytes accessed | tf_op | source)
XLA Modules:
  0.0 29.9 jit_solution(4539142091171873271)
XLA Ops:
  1.9 0.0 copy-start
  1.9 0.0 copy-start.1
  1.9 0.0 copy-start.2
  2.0 27.2 %shard_map.103 = (f32[16,16,128]{2,1,0:T(8,128)S(1)}, f32[16,16,128]{2,1,0:T(8,128)S(1)}, f32[1,1,128]{2,1,0:T(1,128)S(1)}, f32[1,1,128]{2,1,0:T(1,128)S(1)}) custom-call(f32[16,16,128]{2,1,0:T(8,128)} %res_hbm.1, f32[16,16,128]{2,1,0:T(8,128)} %dir_hbm.1, f32[1,1]{1,0:T(1,128)} %bitcast.4.rz_hbm, s32[2,16,16]{2,1,0:T(8,128)} %wall_hbm.1, ...), custom_call_target="tpu_custom_call" | custom-call | tf_op jit(solution)/shard_map/pallas_call | solution.py:272
  29.2 0.0 copy-done
  29.2 0.0 copy-done.1
  29.2 0.0 copy-done.2
  29.2 0.8 %multiply_add_fusion = (f32[16,16,128]{2,1,0:T(8,128)}, f32[16,16,128]{2,1,0:T(8,128)}, f32[16,16,128]{2,1,0:T(8,128)}) fusion(f32[16,16,128]{2,1,0:T(8,128)S(1)} %get-tuple-element.9, f32[16,16,128]{2,1,0:T(8,128)S(1)} %copy-done.1, f32[128]{0:T(128)S(1)} %bitcast.7, f32[16,16,128]{2,1,0:T(8,128)S(1)} %copy-done.2, f32[128]{0:T(128)S(1)} %bitcast.6, ...), kind=kLoop, calls=%fused_computation | loop fusion | flops 196608 | bytes 1049600 | tf_op jit(solution)/shard_map/add | solution.py:310
Async XLA Ops:
  1.9 27.2 %copy-start = (f32[16,16,128]{2,1,0:T(8,128)S(1)}, f32[16,16,128]{2,1,0:T(8,128)}, u32[]{:S(2)}) copy-start(f32[16,16,128]{2,1,0:T(8,128)} %res_hbm.1) | copy-start | bytes 393220
  1.9 27.2 %copy-start.1 = (f32[16,16,128]{2,1,0:T(8,128)S(1)}, f32[16,16,128]{2,1,0:T(8,128)}, u32[]{:S(2)}) copy-start(f32[16,16,128]{2,1,0:T(8,128)} %dir_hbm.1) | copy-start | bytes 393220
  1.9 27.2 %copy-start.2 = (f32[16,16,128]{2,1,0:T(8,128)S(1)}, f32[16,16,128]{2,1,0:T(8,128)}, u32[]{:S(2)}) copy-start(f32[16,16,128]{2,1,0:T(8,128)} %param.8) | copy-start | bytes 393220

commit v4 on v3

--- a/solution.py
+++ b/solution.py
@@ -49,30 +49,32 @@
     res_hbm, dir_hbm, rz_hbm, wall_hbm, own_hbm, basis_hbm, inv_hbm,
     app, precond, step_row, ratio_row,
     res, dirn, rz, wall, own, basis, inv,
-    low_face, high_face, halo_buf, inv_diag, w_res, w_app, group_sum, per_cell, part_res, v_ref,
+    low_face, high_face, halo_buf, inv_diag, w_all, w_faces, w_rows, edge, group_sum, per_cell, early, v_ref,
     line_buf, plane_buf,
     in_sem, basis_sem, halo_send, halo_recv, line_send, line_recv, plane_send, plane_recv,
 ):
     halo, line, plane, line_me, plane_me, z = places()
-    barrier = pltpu.get_barrier_semaphore()
-    for peer in line[:2] + plane[:1] + line[2:6] + plane[1:5] + halo[:2] + line[6:10] + plane[5:] + line[10:] + halo[2:]:
-        pl.semaphore_signal(barrier, inc=1, device_id=peer, device_id_type=MESH)
     loads = [
         pltpu.make_async_copy(src, dst, in_sem.at[i])
         for i, (src, dst) in enumerate(
             ((dir_hbm, dirn), (wall_hbm, wall), (res_hbm, res), (rz_hbm, rz), (own_hbm, own), (inv_hbm, inv))
         )
     ]
+    loads[0].start()
+    barrier = pltpu.get_barrier_semaphore()
+    for peer in line[:2] + plane[:1] + line[2:6] + plane[1:5] + halo[:2] + line[6:10] + plane[5:] + line[10:] + halo[2:]:
+        pl.semaphore_signal(barrier, inc=1, device_id=peer, device_id_type=MESH)
     basis_loads = [
         pltpu.make_async_copy(basis_hbm.at[pl.ds(8 * i, 8)], basis.at[pl.ds(8 * i, 8)], basis_sem.at[i])
         for i in range(8)
     ]
-    for load in loads[:5] + basis_loads + loads[5:]:
+    for load in loads[1:5] + basis_loads + loads[5:]:
         load.start()
 
     lane = iota((16, 128), 1)
     row = iota((16, 128), 0)
-    group_sum[...] = (iota((1024, 128), 0) // 16 == iota((1024, 128), 1) % 64).astype(F32).astype(BF16)
+    group_sum[0:1024, :] = (iota((1024, 128), 0) // 16 == iota((1024, 128), 1) % 64).astype(F32).astype(BF16)
+    group_sum[1024:1152, :] = (iota((128, 128), 0) // 2 == iota((128, 128), 1) % 64).astype(F32).astype(BF16)
     per_cell[...] = (iota((128, 1024), 0) % 64 == iota((128, 1024), 1) // 16).astype(F32).astype(BF16)
 
     loads[0].wait()
@@ -114,35 +116,60 @@
         r = res[x]
         sum_rr += r * r * inverse
         r_low = r.astype(BF16)
-        w_res[0:16, 128 * x : 128 * x + 128] = r_low
-        w_res[16:32, 128 * x : 128 * x + 128] = (r - r_low.astype(F32)).astype(BF16)
-
-    pick = iota((32, 1024), 0) % 16 == iota((32, 1024), 1) % 16
-
-    def slab(pair):
-        return jnp.concatenate(
-            [basis[:, 2 * pair].reshape(1024, 128), basis[:, 2 * pair + 1].reshape(1024, 128)], axis=1
-        )
-
-    def project(weights):
-        total = jnp.zeros((32, 1024), F32)
-        for pair in range(8):
-            total += lax.dot_general(
-                weights[:, 256 * pair : 256 * pair + 256], slab(pair), NT, preferred_element_type=F32
-            )
-        total = jnp.where(pick, total, 0.0)
-        first = jnp.sum(total[0:16], axis=0, keepdims=True)
-        second = jnp.sum(total[16:32], axis=0, keepdims=True)
-        at = iota((8, 1024), 0)
-        both = jnp.where(at == 0, first, jnp.where(at == 1, second, 0.0))
+        at = slice(128 * x, 128 * x + 128)
+        w_all[0:16, at] = r_low
+        w_all[16:32, at] = (r - r_low.astype(F32)).astype(BF16)
+        if 0 < x < 15:
+            inner = jnp.where((row > 0) & (row < 15), app[x], 0.0)
+        else:
+            inner = jnp.zeros((16, 128), F32)
+            w_rows[:, at] = inner.astype(BF16)
+        q_low = inner.astype(BF16)
+        w_all[32:48, at] = q_low
+        w_all[48:64, at] = (inner - q_low.astype(F32)).astype(BF16)
+
+    pick = iota((64, 1024), 0) % 16 == iota((64, 1024), 1) % 16
+
+    def slab(low, high):
+        return jnp.concatenate([basis[:, low].reshape(1024, 128), basis[:, high].reshape(1024, 128)], axis=1)
+
+    def picked(total):
+        total = jnp.where(pick[0 : total.shape[0]], total, 0.0)
+        return [jnp.sum(total[16 * i : 16 * i + 16], axis=0, keepdims=True) for i in range(total.shape[0] // 16)]
+
+    def stack(lines):
+        at = iota((8, lines[0].shape[1]), 0)
+        total = jnp.zeros(at.shape, F32)
+        for i, line in enumerate(lines):
+            total = jnp.where(at == i, line, total)
+        return total
+
+    def by_basis(both, groups):
         one, two, three = (part.astype(F32) for part in split3(both))
         stacked = jnp.concatenate([one, two, three, jnp.zeros_like(one)], axis=0).astype(BF16)
-        sums = jnp.dot(stacked, group_sum[...], preferred_element_type=F32)
+        sums = jnp.dot(stacked, groups, preferred_element_type=F32)
         return sums[0:8] + sums[8:16] + sums[16:24]
 
     for load in basis_loads:
         load.wait()
-    part_res[...] = project(w_res)
+    total = jnp.zeros((64, 1024), F32)
+    for pair in range(8):
+        total += lax.dot_general(
+            w_all[:, 256 * pair : 256 * pair + 256], slab(2 * pair, 2 * pair + 1), NT, preferred_element_type=F32
+        )
+    early[...] = by_basis(stack(picked(total)), group_sum[0:1024, :])
+    choose = (
+        (iota((32, 256), 0) // 2 == iota((32, 256), 1) // 16)
+        & (iota((32, 256), 1) % 16 == 15 * (iota((32, 256), 0) % 2))
+    ).astype(F32).astype(BF16)
+    for part in range(4):
+        for pair in range(8):
+            tile = jnp.concatenate(
+                [basis[16 * part : 16 * part + 16, 2 * pair + i].reshape(256, 128) for i in range(2)], axis=1
+            )
+            edge[32 * part : 32 * part + 32, 256 * pair : 256 * pair + 256] = jnp.dot(
+                choose, tile, preferred_element_type=F32
+            ).astype(BF16)
 
     for copy in sends:
         copy.wait_recv()
@@ -165,9 +192,24 @@
         sum_rq += res[x] * scaled
         sum_qq += q * scaled
         q_low = q.astype(BF16)
-        w_app[0:16, 128 * x : 128 * x + 128] = q_low
-        w_app[16:32, 128 * x : 128 * x + 128] = (q - q_low.astype(F32)).astype(BF16)
-    part_app = project(w_app)
+        q_rest = q - q_low.astype(F32)
+        if x in (0, 15):
+            at = slice(0, 128) if x == 0 else slice(128, 256)
+            w_faces[0:16, at] = q_low
+            w_faces[16:32, at] = q_rest.astype(BF16)
+        else:
+            q_low = q_low.astype(F32)
+            ends = jnp.where(row == 0, q_low[0:1], jnp.where(row == 1, q_low[15:16], 0.0))
+            ends = jnp.where(row == 2, q_rest[0:1], jnp.where(row == 3, q_rest[15:16], ends))
+            w_rows[:, 128 * x : 128 * x + 128] = ends.astype(BF16)
+    faces = picked(lax.dot_general(w_faces[...], slab(0, 15), NT, preferred_element_type=F32))
+    ends = lax.dot_general(w_rows[...], edge[...], NT, preferred_element_type=F32)
+    ends = jnp.where(row % 2 == lane % 2, ends, 0.0)
+    late = by_basis(
+        jnp.concatenate([stack(faces), stack([ends[0:1] + ends[1:2], ends[2:3] + ends[3:4]])], axis=1), group_sum[...]
+    )
+    part_res = early[...]
+    part_app = part_res[2:4] + late[0:2]
     loads[4].wait()
     lane1 = lane[0:1]
     scalars = own[0, 0].astype(F32) * jnp.where(lane1 == 16 + line_me, 1.0, 0.0)
@@ -257,7 +299,7 @@
     spread = jnp.dot(here, per_cell[...], preferred_element_type=F32)
     spread = jnp.where(pick[0:16], spread, 0.0).astype(BF16)
     for pair in range(8):
-        correction = jnp.dot(spread, slab(pair), preferred_element_type=F32)
+        correction = jnp.dot(spread, slab(2 * pair, 2 * pair + 1), preferred_element_type=F32)
         for side in range(2):
             x = 2 * pair + side
             updated = res[x] - step * app[x]
@@ -286,9 +328,11 @@
             pltpu.VMEM((16, 128), F32),
             pltpu.VMEM((4, 16, 128), F32),
             pltpu.VMEM((16, 16, 128), F32),
-            pltpu.VMEM((32, 2048), BF16),
-            pltpu.VMEM((32, 2048), BF16),
-            pltpu.VMEM((1024, 128), BF16),
+            pltpu.VMEM((64, 2048), BF16),
+            pltpu.VMEM((32, 256), BF16),
+            pltpu.VMEM((16, 2048), BF16),
+            pltpu.VMEM((128, 2048), BF16),
+            pltpu.VMEM((1152, 128), BF16),
             pltpu.VMEM((128, 1024), BF16),
             pltpu.VMEM((8, 128), F32),
             pltpu.VMEM((8, 128), F32),

time: 30 us -> 29.2 us (0.973)
  Pallas kernels: 27.2 us -> 26.4 us
    pallas_call x1, Pallas kernels: 27.2 us -> 26.4 us  [on_device(): pl.pallas_call(kernel, out_shape=(block, block, line, line), in_specs=[pl...]
where the time goes in v4:
time: 29.2 us; the launch traced here: 29.1 us
  Pallas kernels  26.4 us (90%)
  between operations  1.98 us (7%)
  other arithmetic  0.76 us (3%)
    pallas_call x1, Pallas kernels, on_device(): pl.pallas_call(kernel, out_shape=(block, block, line, line), in_specs=[pl...  26.4 us
    add x1, other arithmetic, on_device(): precond + ratio * direction  0.76 us

profile of v4, /device:TPU:1, one launch (start us, length us, event | category | flops | bytes accessed | tf_op | source)
XLA Modules:
  0.0 29.1 jit_solution(11236651653200695869)
XLA Ops:
  1.9 0.0 copy-start
  1.9 0.0 copy-start.1
  1.9 0.0 copy-start.2
  2.0 26.4 %shard_map.103 = (f32[16,16,128]{2,1,0:T(8,128)S(1)}, f32[16,16,128]{2,1,0:T(8,128)S(1)}, f32[1,1,128]{2,1,0:T(1,128)S(1)}, f32[1,1,128]{2,1,0:T(1,128)S(1)}) custom-call(f32[16,16,128]{2,1,0:T(8,128)} %res_hbm.1, f32[16,16,128]{2,1,0:T(8,128)} %dir_hbm.1, f32[1,1]{1,0:T(1,128)} %bitcast.4.rz_hbm, s32[2,16,16]{2,1,0:T(8,128)} %wall_hbm.1, ...), custom_call_target="tpu_custom_call" | custom-call | tf_op jit(solution)/shard_map/pallas_call | solution.py:314
  28.3 0.0 copy-done
  28.4 0.0 copy-done.1
  28.4 0.0 copy-done.2
  28.4 0.8 %multiply_add_fusion = (f32[16,16,128]{2,1,0:T(8,128)}, f32[16,16,128]{2,1,0:T(8,128)}, f32[16,16,128]{2,1,0:T(8,128)}) fusion(f32[16,16,128]{2,1,0:T(8,128)S(1)} %get-tuple-element.9, f32[16,16,128]{2,1,0:T(8,128)S(1)} %copy-done.1, f32[128]{0:T(128)S(1)} %bitcast.7, f32[16,16,128]{2,1,0:T(8,128)S(1)} %copy-done.2, f32[128]{0:T(128)S(1)} %bitcast.6, ...), kind=kLoop, calls=%fused_computation | loop fusion | flops 196608 | bytes 1049600 | tf_op jit(solution)/shard_map/add | solution.py:354
Async XLA Ops:
  1.9 26.4 %copy-start = (f32[16,16,128]{2,1,0:T(8,128)S(1)}, f32[16,16,128]{2,1,0:T(8,128)}, u32[]{:S(2)}) copy-start(f32[16,16,128]{2,1,0:T(8,128)} %res_hbm.1) | copy-start | bytes 393220
  1.9 26.4 %copy-start.1 = (f32[16,16,128]{2,1,0:T(8,128)S(1)}, f32[16,16,128]{2,1,0:T(8,128)}, u32[]{:S(2)}) copy-start(f32[16,16,128]{2,1,0:T(8,128)} %dir_hbm.1) | copy-start | bytes 393220
  1.9 26.4 %copy-start.2 = (f32[16,16,128]{2,1,0:T(8,128)S(1)}, f32[16,16,128]{2,1,0:T(8,128)}, u32[]{:S(2)}) copy-start(f32[16,16,128]{2,1,0:T(8,128)} %param.8) | copy-start | bytes 393220

commit v5 on v4

--- a/solution.py
+++ b/solution.py
@@ -81,16 +81,6 @@
     for x in range(16):
         low_face[pl.ds(x, 1), :] = dirn[x, pl.ds(0, 1), :]
         high_face[pl.ds(x, 1), :] = dirn[x, pl.ds(15, 1), :]
-    pl.semaphore_wait(barrier, len(halo + line + plane))
-    sends = []
-    for i, (src, peer) in enumerate(zip((dirn.at[15], dirn.at[0], high_face, low_face), halo)):
-        copy = pltpu.make_async_remote_copy(
-            src_ref=src, dst_ref=halo_buf.at[i], send_sem=halo_send.at[i], recv_sem=halo_recv.at[i],
-            device_id=peer, device_id_type=MESH,
-        )
-        copy.start()
-        sends.append(copy)
-
     loads[1].wait()
     loads[2].wait()
     same = iota((16, 16), 0) == iota((16, 16), 1)
@@ -127,6 +117,16 @@
         q_low = inner.astype(BF16)
         w_all[32:48, at] = q_low
         w_all[48:64, at] = (inner - q_low.astype(F32)).astype(BF16)
+
+    pl.semaphore_wait(barrier, len(halo + line + plane))
+    sends = []
+    for i, (src, peer) in enumerate(zip((dirn.at[15], dirn.at[0], high_face, low_face), halo)):
+        copy = pltpu.make_async_remote_copy(
+            src_ref=src, dst_ref=halo_buf.at[i], send_sem=halo_send.at[i], recv_sem=halo_recv.at[i],
+            device_id=peer, device_id_type=MESH,
+        )
+        copy.start()
+        sends.append(copy)
 
     pick = iota((64, 1024), 0) % 16 == iota((64, 1024), 1) % 16
 
@@ -212,13 +212,15 @@
     part_app = part_res[2:4] + late[0:2]
     loads[4].wait()
     lane1 = lane[0:1]
-    scalars = own[0, 0].astype(F32) * jnp.where(lane1 == 16 + line_me, 1.0, 0.0)
+    scalars = jnp.zeros((1, 128), F32)
     for i, value in enumerate((sum_dq, sum_rr, sum_rq, sum_qq)):
         whole = jnp.sum(jnp.sum(value, axis=0, keepdims=True), axis=1, keepdims=True)
         scalars = jnp.where(lane1 == i, whole, scalars)
     line_buf[line_me, pl.ds(0, 1), :] = jnp.where(lane1 < 64, part_res[0:1, :], part_app[0:1, :])
     line_buf[line_me, pl.ds(1, 1), :] = jnp.where(lane1 < 64, part_res[1:2, :], part_app[1:2, :])
     line_buf[line_me, pl.ds(2, 1), :] = scalars
+    spot = lax.rem(plane_me, 8) * 16 + line_me
+    line_buf[line_me, pl.ds(3, 1), :] = own[0, 0].astype(F32) * jnp.where(lane1 == spot, 1.0, 0.0)
 
     copies = []
     for i, peer in enumerate(line):
@@ -233,7 +235,8 @@
         copy.wait_recv()
     for kind in range(2):
         plane_buf[plane_me, pl.ds(16 * kind, 16), :] = line_buf[:, kind, :]
-    plane_buf[plane_me, pl.ds(32, 1), :] = jnp.sum(line_buf[:, 2, :], axis=0, keepdims=True)
+    for kind in range(2, 4):
+        plane_buf[plane_me, pl.ds(30 + kind, 1), :] = jnp.sum(line_buf[:, kind, :], axis=0, keepdims=True)
     copies = []
     for i, peer in enumerate(plane):
         copy = pltpu.make_async_remote_copy(
@@ -253,10 +256,8 @@
     rz_old = rz[0, 0]
     step = rz_old / totals[:, 0:1]
     step_row[0] = jnp.broadcast_to(step, (1, 128))
-    to_lanes = (iota((128, 256), 0) == 16 + iota((128, 256), 1) % 16).astype(F32).astype(BF16)
-    owners = jnp.dot(jnp.where((lane >= 16) & (lane < 32), scalars, 0.0).astype(BF16), to_lanes, preferred_element_type=F32)
-    owners = jnp.where(iota((16, 256), 0) == iota((16, 256), 1) // 16, owners, 0.0)
-    owners = jnp.sum(owners, axis=0, keepdims=True)
+    owners = plane_buf[:, 33, :]
+    owners = jnp.concatenate([jnp.sum(owners[8 * i : 8 * i + 8], axis=0, keepdims=True) for i in range(2)], axis=1)
     at = iota((16, 256), 0)
     wanted = jnp.where(at < 8, 2 * at, 2 * at - 15).astype(F32)
     chosen = (owners == wanted).astype(F32).astype(BF16)
@@ -336,8 +337,8 @@
             pltpu.VMEM((128, 1024), BF16),
             pltpu.VMEM((8, 128), F32),
             pltpu.VMEM((8, 128), F32),
-            pltpu.VMEM((16, 3, 128), F32),
-            pltpu.VMEM((16, 33, 128), F32),
+            pltpu.VMEM((16, 4, 128), F32),
+            pltpu.VMEM((16, 34, 128), F32),
             pltpu.SemaphoreType.DMA((6,)),
             pltpu.SemaphoreType.DMA((8,)),
             pltpu.SemaphoreType.DMA((4,)),

time: 29.2 us -> 29.2 us (level)
  no operation moved by 1% of the time
where the time goes in v5:
time: 29.2 us; the launch traced here: 29.1 us
  Pallas kernels  26.3 us (90%)
  between operations  1.98 us (7%)
  other arithmetic  0.76 us (3%)
    pallas_call x1, Pallas kernels, on_device(): pl.pallas_call(kernel, out_shape=(block, block, line, line), in_specs=[pl...  26.3 us
    add x1, other arithmetic, on_device(): precond + ratio * direction  0.76 us

profile of v5, /device:TPU:1, one launch (start us, length us, event | category | flops | bytes accessed | tf_op | source)
XLA Modules:
  0.0 29.1 jit_solution(319468104503409221)
XLA Ops:
  1.9 0.0 copy-start
  1.9 0.0 copy-start.1
  1.9 0.0 copy-start.2
  2.0 26.3 %shard_map.103 = (f32[16,16,128]{2,1,0:T(8,128)S(1)}, f32[16,16,128]{2,1,0:T(8,128)S(1)}, f32[1,1,128]{2,1,0:T(1,128)S(1)}, f32[1,1,128]{2,1,0:T(1,128)S(1)}) custom-call(f32[16,16,128]{2,1,0:T(8,128)} %res_hbm.1, f32[16,16,128]{2,1,0:T(8,128)} %dir_hbm.1, f32[1,1]{1,0:T(1,128)} %bitcast.4.rz_hbm, s32[2,16,16]{2,1,0:T(8,128)} %wall_hbm.1, ...), custom_call_target="tpu_custom_call" | custom-call | tf_op jit(solution)/shard_map/pallas_call | solution.py:315
  28.3 0.0 copy-done
  28.3 0.0 copy-done.1
  28.3 0.0 copy-done.2
  28.3 0.8 %multiply_add_fusion = (f32[16,16,128]{2,1,0:T(8,128)}, f32[16,16,128]{2,1,0:T(8,128)}, f32[16,16,128]{2,1,0:T(8,128)}) fusion(f32[16,16,128]{2,1,0:T(8,128)S(1)} %get-tuple-element.9, f32[16,16,128]{2,1,0:T(8,128)S(1)} %copy-done.1, f32[128]{0:T(128)S(1)} %bitcast.7, f32[16,16,128]{2,1,0:T(8,128)S(1)} %copy-done.2, f32[128]{0:T(128)S(1)} %bitcast.6, ...), kind=kLoop, calls=%fused_computation | loop fusion | flops 196608 | bytes 1049600 | tf_op jit(solution)/shard_map/add | solution.py:355
Async XLA Ops:
  1.9 26.4 %copy-start = (f32[16,16,128]{2,1,0:T(8,128)S(1)}, f32[16,16,128]{2,1,0:T(8,128)}, u32[]{:S(2)}) copy-start(f32[16,16,128]{2,1,0:T(8,128)} %res_hbm.1) | copy-start | bytes 393220
  1.9 26.4 %copy-start.1 = (f32[16,16,128]{2,1,0:T(8,128)S(1)}, f32[16,16,128]{2,1,0:T(8,128)}, u32[]{:S(2)}) copy-start(f32[16,16,128]{2,1,0:T(8,128)} %dir_hbm.1) | copy-start | bytes 393220
  1.9 26.4 %copy-start.2 = (f32[16,16,128]{2,1,0:T(8,128)S(1)}, f32[16,16,128]{2,1,0:T(8,128)}, u32[]{:S(2)}) copy-start(f32[16,16,128]{2,1,0:T(8,128)} %param.8) | copy-start | bytes 393220

commit v6 on v5

--- a/solution.py
+++ b/solution.py
@@ -62,7 +62,10 @@
     ]
     loads[0].start()
     barrier = pltpu.get_barrier_semaphore()
-    for peer in line[:2] + plane[:1] + line[2:6] + plane[1:5] + halo[:2] + line[6:10] + plane[5:] + line[10:] + halo[2:]:
+    stream = lax.axis_index("stream")
+    beside = [(lax.rem(stream + 31 + 2 * lax.rem(stream, 2), 32), z)]
+    greeted = line[:2] + plane[:1] + line[2:6] + plane[1:5] + beside + line[6:10] + plane[5:] + line[10:]
+    for peer in greeted:
         pl.semaphore_signal(barrier, inc=1, device_id=peer, device_id_type=MESH)
     basis_loads = [
         pltpu.make_async_copy(basis_hbm.at[pl.ds(8 * i, 8)], basis.at[pl.ds(8 * i, 8)], basis_sem.at[i])
@@ -118,7 +121,7 @@
         w_all[32:48, at] = q_low
         w_all[48:64, at] = (inner - q_low.astype(F32)).astype(BF16)
 
-    pl.semaphore_wait(barrier, len(halo + line + plane))
+    pl.semaphore_wait(barrier, len(greeted))
     sends = []
     for i, (src, peer) in enumerate(zip((dirn.at[15], dirn.at[0], high_face, low_face), halo)):
         copy = pltpu.make_async_remote_copy(

time: 29.2 us -> 29.2 us (level)
  no operation moved by 1% of the time
where the time goes in v6:
time: 29.2 us; the launch traced here: 29.1 us
  Pallas kernels  26.3 us (90%)
  between operations  1.98 us (7%)
  other arithmetic  0.76 us (3%)
    pallas_call x1, Pallas kernels, on_device(): pl.pallas_call(kernel, out_shape=(block, block, line, line), in_specs=[pl...  26.3 us
    add x1, other arithmetic, on_device(): precond + ratio * direction  0.76 us

profile of v6, /device:TPU:1, one launch (start us, length us, event | category | flops | bytes accessed | tf_op | source)
XLA Modules:
  0.0 29.1 jit_solution(14395130679503735885)
XLA Ops:
  1.9 0.0 copy-start
  1.9 0.0 copy-start.1
  1.9 0.0 copy-start.2
  2.0 26.3 %shard_map.103 = (f32[16,16,128]{2,1,0:T(8,128)S(1)}, f32[16,16,128]{2,1,0:T(8,128)S(1)}, f32[1,1,128]{2,1,0:T(1,128)S(1)}, f32[1,1,128]{2,1,0:T(1,128)S(1)}) custom-call(f32[16,16,128]{2,1,0:T(8,128)} %res_hbm.1, f32[16,16,128]{2,1,0:T(8,128)} %dir_hbm.1, f32[1,1]{1,0:T(1,128)} %bitcast.4.rz_hbm, s32[2,16,16]{2,1,0:T(8,128)} %wall_hbm.1, ...), custom_call_target="tpu_custom_call" | custom-call | tf_op jit(solution)/shard_map/pallas_call | solution.py:318
  28.3 0.0 copy-done
  28.3 0.0 copy-done.1
  28.3 0.0 copy-done.2
  28.3 0.8 %multiply_add_fusion = (f32[16,16,128]{2,1,0:T(8,128)}, f32[16,16,128]{2,1,0:T(8,128)}, f32[16,16,128]{2,1,0:T(8,128)}) fusion(f32[16,16,128]{2,1,0:T(8,128)S(1)} %get-tuple-element.9, f32[16,16,128]{2,1,0:T(8,128)S(1)} %copy-done.1, f32[128]{0:T(128)S(1)} %bitcast.7, f32[16,16,128]{2,1,0:T(8,128)S(1)} %copy-done.2, f32[128]{0:T(128)S(1)} %bitcast.6, ...), kind=kLoop, calls=%fused_computation | loop fusion | flops 196608 | bytes 1049600 | tf_op jit(solution)/shard_map/add | solution.py:358
Async XLA Ops:
  1.9 26.4 %copy-start = (f32[16,16,128]{2,1,0:T(8,128)S(1)}, f32[16,16,128]{2,1,0:T(8,128)}, u32[]{:S(2)}) copy-start(f32[16,16,128]{2,1,0:T(8,128)} %res_hbm.1) | copy-start | bytes 393220
  1.9 26.4 %copy-start.1 = (f32[16,16,128]{2,1,0:T(8,128)S(1)}, f32[16,16,128]{2,1,0:T(8,128)}, u32[]{:S(2)}) copy-start(f32[16,16,128]{2,1,0:T(8,128)} %dir_hbm.1) | copy-start | bytes 393220
  1.9 26.4 %copy-start.2 = (f32[16,16,128]{2,1,0:T(8,128)S(1)}, f32[16,16,128]{2,1,0:T(8,128)}, u32[]{:S(2)}) copy-start(f32[16,16,128]{2,1,0:T(8,128)} %param.8) | copy-start | bytes 393220
